TPU v7x, 128 devices: a whole 4x4x4 slice. The times are simulated.
128 devices in a mesh: mesh: 32 (over y, x, core), state: 4 (over z).
Axes of the slice: x: 4, y: 4, z: 4, core: 2. Of those that a mesh axis runs over, the one named last changes fastest.
Arguments:
- kern_blocks: bfloat16 [768, 16, 128, 128], P('mesh'), may hold values from 4.296875e-06 to 0.13744531
- kern_cols: int32 [768, 16], P('mesh'), may hold values from 0 to 767, as said below
- state_kernel: bfloat16 [512, 512], replicated, may hold values from 0 to 0.61, as said below
- start_v: float32 [98304, 512], P('mesh', 'state'), may hold values from 0.5 to 5
- mu: float32 [98304, 512], P(('mesh', 'state')), may hold values from 0.2 to 2
- nu: float32 [98304, 512], P('mesh', 'state'), may hold values from 0.2 to 2
Outputs:
- potential_u: float32 [98304, 512], P(('mesh', 'state'))
- potential_v: float32 [98304, 512], P('mesh', 'state')
Inputs may be any that keep to these rules, and one draw needn't show every extreme that they name: `kern_cols`: each block row names 16 different block columns, its own block among them. The block rows held by index d of mesh (rows d * 24 to (d + 1) * 24 - 1) refer, among the blocks of index d - 1 and d + 1 (wrapping around 32), only to the last 6 blocks of d - 1 and the first 6 blocks of d + 1, and to all of them; among the blocks of every other index, to at most 2 distinct blocks, and to exactly 2 of index d + 2. How many other indices they reach differs from index to index. `state_kernel`: each row has a positive diagonal entry.
All inputs are finite; a program needn't handle non-finite values.
Results may differ from a plain program's by a relative error of at most 0.0033.
Values may be sent and summed in bfloat16 or wider, within the bound.
A program may use at most 192 MiB of HBM per device.

v0:
```python
import jax
import jax.numpy as jnp
from jax import lax
from jax.sharding import PartitionSpec as P

ITERS = 2
CAP = 6


def request_plan(owners, places, remote, peer_count, block_rows, width):
    peer_ids = jnp.arange(peer_count, dtype=jnp.int32)
    place_ids = jnp.arange(block_rows, dtype=jnp.int32)
    matches = (
        remote[:, None, None]
        & (owners[:, None, None] == peer_ids[None, :, None])
        & (places[:, None, None] == place_ids[None, None, :])
    )
    matches = matches.astype(jnp.int32)
    needed = jnp.max(matches, axis=0)
    ranking = jnp.cumsum(needed, axis=1) - needed
    ref_slots = jnp.sum(matches * ranking[None, :, :], axis=(1, 2))
    slot_ids = jnp.arange(width, dtype=jnp.int32)
    selected = needed[:, :, None] * (ranking[:, :, None] == slot_ids[None, None, :]).astype(
        jnp.int32
    )
    requests = jnp.sum(selected * place_ids[None, :, None], axis=1)
    return (ref_slots, requests)


def rounded_sum(values):
    return lax.optimization_barrier(values.astype(jnp.bfloat16)).astype(jnp.float32)


def per_device(kern_blocks, kern_cols, state_kernel, start_v, mu, nu):
    block_rows, degree, block_size, _ = kern_blocks.shape
    local_rows, state_cols = start_v.shape
    peer_count = lax.axis_size("mesh")
    state_count = lax.axis_size("state")
    my_index = lax.axis_index("mesh")
    flat_cols = kern_cols.reshape(-1)
    owners = flat_cols // block_rows
    places = flat_cols % block_rows
    remote = owners != my_index
    ref_slots, requests = request_plan(owners, places, remote, peer_count, block_rows, CAP)
    asked = lax.all_to_all(requests, "mesh", split_axis=0, concat_axis=0, tiled=True)
    sources = jnp.where(remote, block_rows + owners * CAP + ref_slots, places)
    table_size = block_rows + peer_count * CAP
    flat_asked = asked.reshape(-1)
    values = start_v
    potential_u = mu
    for sweep in range(ITERS):
        blocks = values.astype(jnp.bfloat16).reshape(block_rows, block_size, state_cols)
        incoming = lax.all_to_all(blocks[asked], "mesh", split_axis=0, concat_axis=0, tiled=True)
        table = jnp.concatenate([blocks, incoming.reshape(-1, block_size, state_cols)], axis=0)
        picked = table[sources].reshape(block_rows, degree, block_size, state_cols)
        applied = jnp.einsum(
            "rkab,rkbc->rac", kern_blocks, picked, preferred_element_type=jnp.float32
        )
        pieces = applied.astype(jnp.bfloat16).reshape(
            state_count, local_rows // state_count, state_cols
        )
        mixed = jnp.einsum(
            "xrl,jl->xrj",
            lax.all_to_all(pieces, "state", split_axis=0, concat_axis=2, tiled=True),
            state_kernel,
            preferred_element_type=jnp.float32,
        )
        potential_u = mu / mixed[0]
        back_rows = jnp.dot(
            potential_u.astype(jnp.bfloat16), state_kernel, preferred_element_type=jnp.float32
        ).astype(jnp.bfloat16)
        returned = lax.all_to_all(back_rows, "state", split_axis=1, concat_axis=0, tiled=True)
        returned = returned.reshape(block_rows, block_size, state_cols)
        spread = jnp.einsum(
            "rkab,rac->rkbc", kern_blocks, returned, preferred_element_type=jnp.float32
        )
        contrib_table = jax.ops.segment_sum(
            spread.reshape(-1, block_size, state_cols), sources, num_segments=table_size
        )
        own_part = rounded_sum(contrib_table[:block_rows])
        outgoing = (
            contrib_table[block_rows:]
            .reshape(peer_count, CAP, block_size, state_cols)
            .astype(jnp.bfloat16)
        )
        arriving = lax.all_to_all(outgoing, "mesh", split_axis=0, concat_axis=0, tiled=True)
        arriving = arriving.reshape(-1, block_size, state_cols).astype(jnp.float32)
        totals = own_part + jax.ops.segment_sum(arriving, flat_asked, num_segments=block_rows)
        values = nu / totals.reshape(local_rows, state_cols)
    return (potential_u, values)


def solution(mesh):
    placed = (
        P("mesh", None, None, None),
        P("mesh", None),
        P(),
        P("mesh", "state"),
        P(("mesh", "state"), None),
        P("mesh", "state"),
    )
    return jax.shard_map(
        per_device,
        mesh=mesh,
        in_specs=placed,
        out_specs=(P(("mesh", "state"), None), P("mesh", "state")),
        check_vma=False,
    )
```

profile of v0, /device:TPU:0, one launch (start us, length us, event | category | flops | bytes accessed | tf_op | source)
XLA Modules:
  0.0 854.1 jit_solution(14254302515081292741)
XLA Ops:
  0.6 0.8 broadcast_divide_fusion
  1.4 0.7 sign_compare_fusion
  2.2 0.1 rem.49
  2.4 0.1 copy.36
  2.5 0.1 ne.120
  2.7 0.6 fusion.1
  3.4 0.2 reduce_window_sum.11
  3.7 0.7 copy.44
  4.4 7.4 all-to-all-start
  11.8 1.5 convert_element_type.63
  13.3 5.8 all-to-all-done
  19.1 0.1 reshape.347
  19.2 7.9 gather_fusion
  27.1 5.4 all-to-all-start.1
  32.7 0.1 ne.115
  32.8 0.2 fusion.2
  33.1 77.2 %all-to-all-done.1 = bf16[32,6,128,128]{3,2,1,0:T(8,128)(2,1)} async-done(((bf16[32,6,128,128]{3,2,1,0:T(8,128)(2,1)}), bf16[32,6,128,128]{3,2,1,0:T(8,128)(2,1)}, u32[]{:S(2)}, u32[]{:S(2)}) %all-to-all-start.1) | async-done | bytes 6291488 | tf_op jit(solution)/shard_map/all_to_all | solution.py:53
  110.3 6.2 pad_maximum_fusion
  116.5 14.3 %gather_fusion.1 = bf16[384,128,128]{2,1,0:T(8,128)(2,1)} fusion(bf16[216,128,128]{2,1,0:T(8,128)(2,1)} %pad_maximum_fusion, s32[1024]{0:T(1024)S(1)} %pad_clamp_fusion), kind=kCustom, calls=%fused_computation.1 | custom fusion | bytes 25167360 | tf_op jit(solution)/shard_map/gather | solution.py:55
  130.8 11.6 %bitcast_convert_fusion.3 = bf16[24,128,128]{1,2,0:T(8,128)(2,1)S(1)} fusion(bf16[24,16,128,128]{3,2,1,0:T(8,128)(2,1)} %param.6, bf16[24,16,128,128]{3,2,1,0:T(8,128)(2,1)} %bitcast.96), kind=kOutput, calls=%fused_computation.16 | convolution fusion | flops 1611005952 | bytes 25952256 | tf_op jit(solution)/shard_map/rkab,rkbc->rac/dot_general | solution.py:56
  142.4 0.3 copy.45
  142.7 14.6 %all_to_all.94 = bf16[4,768,128]{1,2,0:T(8,128)(2,1)S(1)} all-to-all(bf16[4,768,128]{1,2,0:T(8,128)(2,1)S(1)} %copy.45), channel_id=1, replica_groups=mesh['mesh'=32,'state'=4] {'state'}, dimensions={0} | all-to-all | bytes 1572864 | tf_op jit(solution)/shard_map/all_to_all | solution.py:64
  157.3 2.5 convolution_convert_fusion.1
  159.8 0.4 copy.46
  160.2 12.1 %all_to_all.95 = bf16[768,4,128]{2,0,1:T(8,128)(2,1)S(1)} all-to-all(bf16[768,4,128]{2,0,1:T(8,128)(2,1)S(1)} %copy.46), channel_id=1, replica_groups=mesh['mesh'=32,'state'=4] {'state'}, dimensions={1} | all-to-all | bytes 1572864 | tf_op jit(solution)/shard_map/all_to_all | solution.py:72
  172.2 16.3 %fusion.6 = f32[24,128,16,128]{3,1,2,0:T(8,128)} fusion(bf16[24,128,128,1]{2,1,3,0:T(8,128)(2,1)S(1)} %bitcast.97, bf16[24,16,128,128]{3,2,1,0:T(8,128)(2,1)} %param.6), kind=kOutput, calls=%fused_computation.46 | convolution fusion | flops 1610612736 | bytes 38535168 | tf_op jit(solution)/shard_map/rkab,rac->rkbc/dot_general | solution.py:74
  188.5 24.7 %copy.48 = f32[384,128,128]{2,1,0:T(8,128)} copy(f32[384,128,128]{1,2,0:T(8,128)} %bitcast.84) | data formatting | bytes 50331648 | tf_op jit(solution)/shard_map/reshape | solution.py:78
  213.2 6.8 broadcast.272.clone
  220.0 79.3 %scatter_fusion = f32[216,128,128]{2,1,0:T(8,128)} fusion(f32[216,128,128]{2,1,0:T(8,128)} %broadcast.272.clone, s32[384]{0:T(512)S(1)} %get-tuple-element.3, f32[384,128,128]{2,1,0:T(8,128)} %copy.48), kind=kCustom, calls=%fused_computation.4 | custom fusion | flops 6291456 | bytes 75499008 | tf_op jit(solution)/shard_map/scatter-add | solution.py:77
  299.3 9.8 %convert.10 = bf16[216,128,128]{2,1,0:T(8,128)(2,1)} convert(f32[216,128,128]{2,1,0:T(8,128)} %scatter_fusion) | non-fusion elementwise | flops 3538944 | bytes 21233664 | tf_op jit(solution)/shard_map/convert.5
  309.1 8.0 slice.29
  317.1 9.1 %all-to-all-start.4 = ((bf16[32,6,128,128]{3,2,1,0:T(8,128)(2,1)}), bf16[32,6,128,128]{3,2,1,0:T(8,128)(2,1)}, u32[]{:S(2)}, u32[]{:S(2)}) async-start(bf16[32,6,128,128]{3,2,1,0:T(8,128)(2,1)} %bitcast.91), calls=%async_computation.4 | async-start | bytes 12582912 | tf_op jit(solution)/shard_map/all_to_all | solution.py:86
  326.3 0.5 broadcast.300
  326.8 0.7 reduce.6
  327.5 0.1 reshape.387
  327.6 0.2 convert_element_type.68
  327.8 76.3 %all-to-all-done.4 = bf16[32,6,128,128]{3,2,1,0:T(8,128)(2,1)} async-done(((bf16[32,6,128,128]{3,2,1,0:T(8,128)(2,1)}), bf16[32,6,128,128]{3,2,1,0:T(8,128)(2,1)}, u32[]{:S(2)}, u32[]{:S(2)}) %all-to-all-start.4) | async-done | bytes 6291488 | tf_op jit(solution)/shard_map/all_to_all | solution.py:86
  404.1 8.9 %bitcast_convert_fusion.1 = f32[192,128,128]{2,1,0:T(8,128)} fusion(bf16[32,6,128,128]{3,2,1,0:T(8,128)(2,1)} %all-to-all-done.4), kind=kLoop, calls=%fused_computation.11 | loop fusion | flops 3145728 | bytes 18874368 | tf_op jit(solution)/shard_map/convert_element_type | solution.py:87
  412.9 25.3 %scatter_fusion.1 = f32[24,128,128]{2,1,0:T(8,128)S(1)} fusion(f32[24,128,128]{2,1,0:T(8,128)S(1)} %convert_element_type.68, s32[192]{0:T(256)S(1)} %reshape.387, f32[192,128,128]{2,1,0:T(8,128)} %bitcast_convert_fusion.1), kind=kCustom, calls=%fused_computation.5 | custom fusion | flops 3145728 | bytes 37749504 | tf_op jit(solution)/shard_map/scatter-add | solution.py:88
  438.2 1.6 fusion
  439.8 7.9 gather_fusion.2
  447.8 77.9 %all_to_all.96 = bf16[32,6,128,128]{3,2,1,0:T(8,128)(2,1)S(1)} all-to-all(bf16[32,6,128,128]{3,2,1,0:T(8,128)(2,1)} %bitcast.94), channel_id=1, replica_groups=mesh['mesh'=32,'state'=4] {'mesh'}, dimensions={0} | all-to-all | bytes 12582912 | tf_op jit(solution)/shard_map/all_to_all | solution.py:53
  525.6 3.5 pad_maximum_fusion.1
  529.1 14.3 %gather_fusion.3 = bf16[384,128,128]{2,1,0:T(8,128)(2,1)} fusion(bf16[216,128,128]{2,1,0:T(8,128)(2,1)} %pad_maximum_fusion.1, s32[1024]{0:T(1024)S(1)} %pad_clamp_fusion), kind=kCustom, calls=%fused_computation.3 | custom fusion | bytes 25167360 | tf_op jit(solution)/shard_map/gather | solution.py:55
  543.4 11.6 %bitcast_convert_fusion.2 = bf16[24,128,128]{1,2,0:T(8,128)(2,1)S(1)} fusion(bf16[24,16,128,128]{3,2,1,0:T(8,128)(2,1)} %param.6, bf16[24,16,128,128]{3,2,1,0:T(8,128)(2,1)} %bitcast.95), kind=kOutput, calls=%fused_computation.13 | convolution fusion | flops 1611005952 | bytes 25952256 | tf_op jit(solution)/shard_map/rkab,rkbc->rac/dot_general | solution.py:56
  555.0 0.3 copy.49
  555.3 15.3 %all_to_all.97 = bf16[4,768,128]{1,2,0:T(8,128)(2,1)S(1)} all-to-all(bf16[4,768,128]{1,2,0:T(8,128)(2,1)S(1)} %copy.49), channel_id=1, replica_groups=mesh['mesh'=32,'state'=4] {'state'}, dimensions={0} | all-to-all | bytes 1572864 | tf_op jit(solution)/shard_map/all_to_all | solution.py:64
  570.5 2.1 convolution_divide_fusion
  572.6 0.6 convolution_convert_fusion
  573.3 0.5 copy-done.1
  573.8 0.4 copy.50
  574.1 14.7 %all_to_all.98 = bf16[768,4,128]{2,0,1:T(8,128)(2,1)S(1)} all-to-all(bf16[768,4,128]{2,0,1:T(8,128)(2,1)S(1)} %copy.50), channel_id=1, replica_groups=mesh['mesh'=32,'state'=4] {'state'}, dimensions={1} | all-to-all | bytes 1572864 | tf_op jit(solution)/shard_map/all_to_all | solution.py:72
  588.8 16.3 %fusion.7 = f32[24,128,16,128]{3,1,2,0:T(8,128)} fusion(bf16[24,128,128,1]{2,1,3,0:T(8,128)(2,1)S(1)} %bitcast.98, bf16[24,16,128,128]{3,2,1,0:T(8,128)(2,1)} %param.6), kind=kOutput, calls=%fused_computation.47 | convolution fusion | flops 1610612736 | bytes 38535168 | tf_op jit(solution)/shard_map/rkab,rac->rkbc/dot_general | solution.py:74
  605.2 24.7 %copy.52 = f32[384,128,128]{2,1,0:T(8,128)} copy(f32[384,128,128]{1,2,0:T(8,128)} %bitcast.85) | data formatting | bytes 50331648 | tf_op jit(solution)/shard_map/reshape | solution.py:78
  629.8 6.8 broadcast.272
  636.7 79.3 %scatter_fusion.2 = f32[216,128,128]{2,1,0:T(8,128)} fusion(f32[216,128,128]{2,1,0:T(8,128)} %broadcast.272, s32[384]{0:T(512)S(1)} %get-tuple-element.3, f32[384,128,128]{2,1,0:T(8,128)} %copy.52), kind=kCustom, calls=%fused_computation.6 | custom fusion | flops 6291456 | bytes 75499008 | tf_op jit(solution)/shard_map/scatter-add | solution.py:77
  716.0 9.8 %convert.11 = bf16[216,128,128]{2,1,0:T(8,128)(2,1)} convert(f32[216,128,128]{2,1,0:T(8,128)} %scatter_fusion.2) | non-fusion elementwise | flops 3538944 | bytes 21233664 | tf_op jit(solution)/shard_map/convert.3
  725.7 8.0 slice.31
  733.8 5.0 all-to-all-start.8
  738.8 0.2 convert_element_type.77
  739.0 77.7 %all-to-all-done.8 = bf16[32,6,128,128]{3,2,1,0:T(8,128)(2,1)} async-done(((bf16[32,6,128,128]{3,2,1,0:T(8,128)(2,1)}), bf16[32,6,128,128]{3,2,1,0:T(8,128)(2,1)}, u32[]{:S(2)}, u32[]{:S(2)}) %all-to-all-start.8) | async-done | bytes 6291488 | tf_op jit(solution)/shard_map/all_to_all | solution.py:86
  816.7 8.9 %bitcast_convert_fusion = f32[192,128,128]{2,1,0:T(8,128)} fusion(bf16[32,6,128,128]{3,2,1,0:T(8,128)(2,1)} %all-to-all-done.8), kind=kLoop, calls=%fused_computation.10 | loop fusion | flops 3145728 | bytes 18874368 | tf_op jit(solution)/shard_map/convert_element_type | solution.py:87
  825.6 25.3 %scatter_fusion.3 = f32[24,128,128]{2,1,0:T(8,128)S(1)} fusion(f32[24,128,128]{2,1,0:T(8,128)S(1)} %convert_element_type.77, s32[192]{0:T(256)S(1)} %reshape.387, f32[192,128,128]{2,1,0:T(8,128)} %bitcast_convert_fusion), kind=kCustom, calls=%fused_computation.7 | custom fusion | flops 3145728 | bytes 37749504 | tf_op jit(solution)/shard_map/scatter-add | solution.py:88
  850.9 2.8 bitcast_divide_fusion
  (24 shorter events, 0.7 us)
Async XLA Ops:
  0.6 156.7 %copy-start = (bf16[512,512]{1,0:T(8,128)(2,1)S(1)}, bf16[512,512]{1,0:T(8,128)(2,1)}, u32[]{:S(2)}) copy-start(bf16[512,512]{1,0:T(8,128)(2,1)} %param.8) | copy-start | bytes 1572868
  4.4 14.7 %all-to-all-start = ((s32[32,1,6]{2,1,0:T(1,128)}), s32[32,1,6]{2,1,0:T(1,128)S(1)}, u32[]{:S(2)}, u32[]{:S(2)}) async-start(s32[32,1,6]{2,1,0:T(1,128)} %copy.44), calls=%async_computation | async-start | bytes 32768 | tf_op jit(solution)/shard_map/all_to_all | solution.py:45
  27.1 83.2 %all-to-all-start.1 = ((bf16[32,6,128,128]{3,2,1,0:T(8,128)(2,1)}), bf16[32,6,128,128]{3,2,1,0:T(8,128)(2,1)}, u32[]{:S(2)}, u32[]{:S(2)}) async-start(bf16[32,6,128,128]{3,2,1,0:T(8,128)(2,1)} %bitcast.90), calls=%async_computation.1 | async-start | bytes 12582912 | tf_op jit(solution)/shard_map/all_to_all | solution.py:53
  317.1 10.4 %slice-start = ((bf16[216,128,128]{2,1,0:T(8,128)(2,1)}), bf16[24,128,128]{2,1,0:T(8,128)(2,1)S(1)}, s32[]{:S(2)}) async-start(bf16[216,128,128]{2,1,0:T(8,128)(2,1)} %convert.10), calls=%async_computation.9 | async-start | bytes 1572864 | tf_op jit(solution)/shard_map/slice | solution.py:80
  317.1 86.9 %all-to-all-start.4 = ((bf16[32,6,128,128]{3,2,1,0:T(8,128)(2,1)}), bf16[32,6,128,128]{3,2,1,0:T(8,128)(2,1)}, u32[]{:S(2)}, u32[]{:S(2)}) async-start(bf16[32,6,128,128]{3,2,1,0:T(8,128)(2,1)} %bitcast.91), calls=%async_computation.4 | async-start | bytes 12582912 | tf_op jit(solution)/shard_map/all_to_all | solution.py:86
  572.6 1.1 copy-start.1
  733.8 5.1 slice-start.1
  733.8 83.0 %all-to-all-start.8 = ((bf16[32,6,128,128]{3,2,1,0:T(8,128)(2,1)}), bf16[32,6,128,128]{3,2,1,0:T(8,128)(2,1)}, u32[]{:S(2)}, u32[]{:S(2)}) async-start(bf16[32,6,128,128]{3,2,1,0:T(8,128)(2,1)} %bitcast.92), calls=%async_computation.8 | async-start | bytes 12582912 | tf_op jit(solution)/shard_map/all_to_all | solution.py:86
where the time goes:
time: 862 us; the launch traced here: 854 us
  other arithmetic  266 us (31%)
  waiting for transfers between devices  237 us (27%)
  blocking collectives  134 us (16%)
  local copies, waits for them, and re-layouts  128 us (15%)
  matrix products  61 us (7%)
  starting transfers between devices  27 us (3%)
    scatter-add x2, other arithmetic, per_device(): jax.ops.segment_sum(spread.reshape(-1, block_size, state_cols), sources,...  159 us
    all_to_all x2, waiting for transfers between devices, per_device(): lax.all_to_all(outgoing, 'mesh', split_axis=0, concat_axis=0, tiled=True)  154 us
    all_to_all x1, blocking collectives, per_device(): lax.all_to_all(blocks[asked], 'mesh', split_axis=0, concat_axis=0, tiled=...  77.9 us
    all_to_all x1, waiting for transfers between devices, per_device(): lax.all_to_all(blocks[asked], 'mesh', split_axis=0, concat_axis=0, tiled=...  77.2 us
    scatter-add x2, other arithmetic, per_device(): jax.ops.segment_sum(arriving, flat_asked, num_segments=block_rows)  50.5 us
    reshape x2, local copies, waits for them, and re-layouts, per_device(): spread.reshape(-1, block_size, state_cols)  49.3 us
    dot_general x2, matrix products, per_device(): jnp.einsum('rkab,rac->rkbc', kern_blocks, returned, preferred_element_typ...  32.7 us
    all_to_all x2, blocking collectives, per_device(): lax.all_to_all(pieces, 'state', split_axis=0, concat_axis=2, tiled=True)  29.9 us
  transfers between devices with their start and end apart: 4, of which 4 were waited for; matrix products, arithmetic and copies ran while one was open for 0% of the time, Pallas kernels for 0%

commit v1 on v0

--- a/solution.py
+++ b/solution.py
@@ -5,6 +5,13 @@
 
 ITERS = 2
 CAP = 6
+
+
+def trade_parts(value, mesh_axis, split, join):
+    devices = lax.axis_size(mesh_axis)
+    blocks = jnp.stack(jnp.split(value, devices, axis=split), axis=0)
+    blocks = lax.all_to_all(blocks, mesh_axis, split_axis=0, concat_axis=0)
+    return jnp.concatenate(blocks, axis=join)
 
 
 def request_plan(owners, places, remote, peer_count, block_rows, width):
@@ -61,7 +68,7 @@
         )
         mixed = jnp.einsum(
             "xrl,jl->xrj",
-            lax.all_to_all(pieces, "state", split_axis=0, concat_axis=2, tiled=True),
+            trade_parts(pieces, "state", 0, 2),
             state_kernel,
             preferred_element_type=jnp.float32,
         )

time: 862 us -> 863 us (level)
    another operation x2 -> x4, other arithmetic: 19.5 us -> 19.7 us
where the time goes in v1:
time: 863 us; the launch traced here: 855 us
  other arithmetic  266 us (31%)
  waiting for transfers between devices  237 us (27%)
  blocking collectives  134 us (16%)
  local copies, waits for them, and re-layouts  128 us (15%)
  matrix products  61 us (7%)
  starting transfers between devices  27 us (3%)
    scatter-add x2, other arithmetic, per_device(): jax.ops.segment_sum(spread.reshape(-1, block_size, state_cols), sources,...  159 us
    all_to_all x2, waiting for transfers between devices, per_device(): lax.all_to_all(outgoing, 'mesh', split_axis=0, concat_axis=0, tiled=True)  154 us
    all_to_all x1, blocking collectives, per_device(): lax.all_to_all(blocks[asked], 'mesh', split_axis=0, concat_axis=0, tiled=...  77.9 us
    all_to_all x1, waiting for transfers between devices, per_device(): lax.all_to_all(blocks[asked], 'mesh', split_axis=0, concat_axis=0, tiled=...  77.2 us
    scatter-add x2, other arithmetic, per_device(): jax.ops.segment_sum(arriving, flat_asked, num_segments=block_rows)  50.5 us
    reshape x2, local copies, waits for them, and re-layouts, per_device(): spread.reshape(-1, block_size, state_cols)  49.3 us
    dot_general x2, matrix products, per_device(): jnp.einsum('rkab,rac->rkbc', kern_blocks, returned, preferred_element_typ...  32.7 us
    all_to_all x2, blocking collectives, trade_parts(): blocks = lax.all_to_all(blocks, mesh_axis, split_axis=0, concat_axis=0)  29.9 us
  transfers between devices with their start and end apart: 4, of which 4 were waited for; matrix products, arithmetic and copies ran while one was open for 0% of the time, Pallas kernels for 0%

profile of v1, /device:TPU:0, one launch (start us, length us, event | category | flops | bytes accessed | tf_op | source)
XLA Modules:
  0.0 855.1 jit_solution(6568671776467171781)
XLA Ops:
  0.6 0.8 broadcast_divide_fusion
  1.4 0.7 sign_compare_fusion
  2.7 0.6 fusion.3
  3.4 0.2 reduce_window_sum.11
  3.7 0.7 copy.58
  4.4 7.4 all-to-all-start
  11.8 1.5 convert_element_type.63
  13.3 5.8 all-to-all-done
  19.2 7.9 gather_fusion
  27.1 5.4 all-to-all-start.1
  32.8 0.2 fusion.4
  33.1 77.2 %all-to-all-done.1 = bf16[32,6,128,128]{3,2,1,0:T(8,128)(2,1)} async-done(((bf16[32,6,128,128]{3,2,1,0:T(8,128)(2,1)}), bf16[32,6,128,128]{3,2,1,0:T(8,128)(2,1)}, u32[]{:S(2)}, u32[]{:S(2)}) %all-to-all-start.1) | async-done | bytes 6291488 | tf_op jit(solution)/shard_map/all_to_all | solution.py:60
  110.3 6.2 pad_maximum_fusion
  116.5 14.3 %gather_fusion.1 = bf16[384,128,128]{2,1,0:T(8,128)(2,1)} fusion(bf16[216,128,128]{2,1,0:T(8,128)(2,1)} %pad_maximum_fusion, s32[1024]{0:T(1024)S(1)} %pad_clamp_fusion), kind=kCustom, calls=%fused_computation.1 | custom fusion | bytes 25167360 | tf_op jit(solution)/shard_map/gather | solution.py:62
  130.8 11.6 %fusion.1 = bf16[24,128,128]{2,1,0:T(8,128)(2,1)S(1)} fusion(bf16[24,16,128,128]{3,2,1,0:T(8,128)(2,1)} %param.6, bf16[24,16,128,128]{3,2,1,0:T(8,128)(2,1)} %bitcast.106), kind=kOutput, calls=%fused_computation.23 | convolution fusion | flops 1611005952 | bytes 25952256 | tf_op jit(solution)/shard_map/rkab,rkbc->rac/dot_general | solution.py:63
  142.5 0.1 copy.59
  142.6 0.1 copy.60
  142.8 0.1 copy.61
  142.9 0.1 copy.62
  143.2 14.6 %all_to_all.74 = bf16[4,1,768,128]{2,3,1,0:T(8,128)(2,1)S(1)} all-to-all(bf16[4,1,768,128]{2,3,1,0:T(8,128)(2,1)S(1)} %pad_maximum_fusion.2), channel_id=1, replica_groups=mesh['mesh'=32,'state'=4] {'state'}, dimensions={0} | all-to-all | bytes 1572864 | tf_op jit(solution)/shard_map/all_to_all | solution.py:13
  157.8 2.4 convolution_convert_fusion.1
  160.3 0.4 copy.64
  160.6 12.1 %all_to_all.75 = bf16[768,4,128]{2,0,1:T(8,128)(2,1)S(1)} all-to-all(bf16[768,4,128]{2,0,1:T(8,128)(2,1)S(1)} %copy.64), channel_id=1, replica_groups=mesh['mesh'=32,'state'=4] {'state'}, dimensions={1} | all-to-all | bytes 1572864 | tf_op jit(solution)/shard_map/all_to_all | solution.py:79
  172.7 16.3 %fusion.10 = f32[24,128,16,128]{3,1,2,0:T(8,128)} fusion(bf16[24,128,128,1]{2,1,3,0:T(8,128)(2,1)S(1)} %bitcast.107, bf16[24,16,128,128]{3,2,1,0:T(8,128)(2,1)} %param.6), kind=kOutput, calls=%fused_computation.52 | convolution fusion | flops 1610612736 | bytes 38535168 | tf_op jit(solution)/shard_map/rkab,rac->rkbc/dot_general | solution.py:81
  189.0 24.7 %copy.66 = f32[384,128,128]{2,1,0:T(8,128)} copy(f32[384,128,128]{1,2,0:T(8,128)} %bitcast.94) | data formatting | bytes 50331648 | tf_op jit(solution)/shard_map/reshape | solution.py:85
  213.7 6.8 broadcast.272.clone
  220.5 79.3 %scatter_fusion = f32[216,128,128]{2,1,0:T(8,128)} fusion(f32[216,128,128]{2,1,0:T(8,128)} %broadcast.272.clone, s32[384]{0:T(512)S(1)} %get-tuple-element.3, f32[384,128,128]{2,1,0:T(8,128)} %copy.66), kind=kCustom, calls=%fused_computation.4 | custom fusion | flops 6291456 | bytes 75499008 | tf_op jit(solution)/shard_map/scatter-add | solution.py:84
  299.8 9.8 %convert.10 = bf16[216,128,128]{2,1,0:T(8,128)(2,1)} convert(f32[216,128,128]{2,1,0:T(8,128)} %scatter_fusion) | non-fusion elementwise | flops 3538944 | bytes 21233664 | tf_op jit(solution)/shard_map/convert.5
  309.6 8.0 slice.37
  317.6 9.1 %all-to-all-start.4 = ((bf16[32,6,128,128]{3,2,1,0:T(8,128)(2,1)}), bf16[32,6,128,128]{3,2,1,0:T(8,128)(2,1)}, u32[]{:S(2)}, u32[]{:S(2)}) async-start(bf16[32,6,128,128]{3,2,1,0:T(8,128)(2,1)} %bitcast.101), calls=%async_computation.4 | async-start | bytes 12582912 | tf_op jit(solution)/shard_map/all_to_all | solution.py:93
  326.7 0.5 broadcast.300
  327.2 0.7 reduce.6
  328.1 0.2 convert_element_type.68
  328.2 76.3 %all-to-all-done.4 = bf16[32,6,128,128]{3,2,1,0:T(8,128)(2,1)} async-done(((bf16[32,6,128,128]{3,2,1,0:T(8,128)(2,1)}), bf16[32,6,128,128]{3,2,1,0:T(8,128)(2,1)}, u32[]{:S(2)}, u32[]{:S(2)}) %all-to-all-start.4) | async-done | bytes 6291488 | tf_op jit(solution)/shard_map/all_to_all | solution.py:93
  404.6 8.9 %bitcast_convert_fusion.1 = f32[192,128,128]{2,1,0:T(8,128)} fusion(bf16[32,6,128,128]{3,2,1,0:T(8,128)(2,1)} %all-to-all-done.4), kind=kLoop, calls=%fused_computation.11 | loop fusion | flops 3145728 | bytes 18874368 | tf_op jit(solution)/shard_map/convert_element_type | solution.py:94
  413.4 25.3 %scatter_fusion.1 = f32[24,128,128]{2,1,0:T(8,128)S(1)} fusion(f32[24,128,128]{2,1,0:T(8,128)S(1)} %convert_element_type.68, s32[192]{0:T(256)S(1)} %reshape.407, f32[192,128,128]{2,1,0:T(8,128)} %bitcast_convert_fusion.1), kind=kCustom, calls=%fused_computation.5 | custom fusion | flops 3145728 | bytes 37749504 | tf_op jit(solution)/shard_map/scatter-add | solution.py:95
  438.7 1.6 fusion
  440.3 7.9 gather_fusion.2
  448.2 77.9 %all_to_all.76 = bf16[32,6,128,128]{3,2,1,0:T(8,128)(2,1)S(1)} all-to-all(bf16[32,6,128,128]{3,2,1,0:T(8,128)(2,1)} %bitcast.104), channel_id=1, replica_groups=mesh['mesh'=32,'state'=4] {'mesh'}, dimensions={0} | all-to-all | bytes 12582912 | tf_op jit(solution)/shard_map/all_to_all | solution.py:60
  526.1 3.5 pad_maximum_fusion.1
  529.6 14.3 %gather_fusion.3 = bf16[384,128,128]{2,1,0:T(8,128)(2,1)} fusion(bf16[216,128,128]{2,1,0:T(8,128)(2,1)} %pad_maximum_fusion.1, s32[1024]{0:T(1024)S(1)} %pad_clamp_fusion), kind=kCustom, calls=%fused_computation.3 | custom fusion | bytes 25167360 | tf_op jit(solution)/shard_map/gather | solution.py:62
  543.9 11.6 %fusion.2 = bf16[24,128,128]{2,1,0:T(8,128)(2,1)S(1)} fusion(bf16[24,16,128,128]{3,2,1,0:T(8,128)(2,1)} %param.6, bf16[24,16,128,128]{3,2,1,0:T(8,128)(2,1)} %bitcast.105), kind=kOutput, calls=%fused_computation.24 | convolution fusion | flops 1611005952 | bytes 25952256 | tf_op jit(solution)/shard_map/rkab,rkbc->rac/dot_general | solution.py:63
  555.5 0.1 copy.67
  555.7 0.1 copy.68
  555.8 0.1 copy.69
  556.0 0.1 copy.70
  556.3 15.3 %all_to_all.77 = bf16[4,1,768,128]{2,3,1,0:T(8,128)(2,1)S(1)} all-to-all(bf16[4,1,768,128]{2,3,1,0:T(8,128)(2,1)S(1)} %pad_maximum_fusion.3), channel_id=1, replica_groups=mesh['mesh'=32,'state'=4] {'state'}, dimensions={0} | all-to-all | bytes 1572864 | tf_op jit(solution)/shard_map/all_to_all | solution.py:13
  571.5 2.1 convolution_divide_fusion
  573.6 0.6 convolution_convert_fusion
  574.2 0.5 copy-done.1
  574.7 0.4 copy.72
  575.1 14.7 %all_to_all.78 = bf16[768,4,128]{2,0,1:T(8,128)(2,1)S(1)} all-to-all(bf16[768,4,128]{2,0,1:T(8,128)(2,1)S(1)} %copy.72), channel_id=1, replica_groups=mesh['mesh'=32,'state'=4] {'state'}, dimensions={1} | all-to-all | bytes 1572864 | tf_op jit(solution)/shard_map/all_to_all | solution.py:79
  589.8 16.3 %fusion.11 = f32[24,128,16,128]{3,1,2,0:T(8,128)} fusion(bf16[24,128,128,1]{2,1,3,0:T(8,128)(2,1)S(1)} %bitcast.108, bf16[24,16,128,128]{3,2,1,0:T(8,128)(2,1)} %param.6), kind=kOutput, calls=%fused_computation.53 | convolution fusion | flops 1610612736 | bytes 38535168 | tf_op jit(solution)/shard_map/rkab,rac->rkbc/dot_general | solution.py:81
  606.1 24.7 %copy.74 = f32[384,128,128]{2,1,0:T(8,128)} copy(f32[384,128,128]{1,2,0:T(8,128)} %bitcast.95) | data formatting | bytes 50331648 | tf_op jit(solution)/shard_map/reshape | solution.py:85
  630.8 6.8 broadcast.272
  637.6 79.3 %scatter_fusion.2 = f32[216,128,128]{2,1,0:T(8,128)} fusion(f32[216,128,128]{2,1,0:T(8,128)} %broadcast.272, s32[384]{0:T(512)S(1)} %get-tuple-element.3, f32[384,128,128]{2,1,0:T(8,128)} %copy.74), kind=kCustom, calls=%fused_computation.6 | custom fusion | flops 6291456 | bytes 75499008 | tf_op jit(solution)/shard_map/scatter-add | solution.py:84
  716.9 9.8 %convert.11 = bf16[216,128,128]{2,1,0:T(8,128)(2,1)} convert(f32[216,128,128]{2,1,0:T(8,128)} %scatter_fusion.2) | non-fusion elementwise | flops 3538944 | bytes 21233664 | tf_op jit(solution)/shard_map/convert.3
  726.7 8.0 slice.39
  734.7 5.0 all-to-all-start.8
  739.8 0.2 convert_element_type.77
  740.0 77.7 %all-to-all-done.8 = bf16[32,6,128,128]{3,2,1,0:T(8,128)(2,1)} async-done(((bf16[32,6,128,128]{3,2,1,0:T(8,128)(2,1)}), bf16[32,6,128,128]{3,2,1,0:T(8,128)(2,1)}, u32[]{:S(2)}, u32[]{:S(2)}) %all-to-all-start.8) | async-done | bytes 6291488 | tf_op jit(solution)/shard_map/all_to_all | solution.py:93
  817.7 8.9 %bitcast_convert_fusion = f32[192,128,128]{2,1,0:T(8,128)} fusion(bf16[32,6,128,128]{3,2,1,0:T(8,128)(2,1)} %all-to-all-done.8), kind=kLoop, calls=%fused_computation.10 | loop fusion | flops 3145728 | bytes 18874368 | tf_op jit(solution)/shard_map/convert_element_type | solution.py:94
  826.6 25.3 %scatter_fusion.3 = f32[24,128,128]{2,1,0:T(8,128)S(1)} fusion(f32[24,128,128]{2,1,0:T(8,128)S(1)} %convert_element_type.77, s32[192]{0:T(256)S(1)} %reshape.407, f32[192,128,128]{2,1,0:T(8,128)} %bitcast_convert_fusion), kind=kCustom, calls=%fused_computation.7 | custom fusion | flops 3145728 | bytes 37749504 | tf_op jit(solution)/shard_map/scatter-add | solution.py:95
  851.8 2.8 bitcast_divide_fusion
  (34 shorter events, 1.5 us)
Async XLA Ops:
  0.6 157.2 %copy-start = (bf16[512,512]{1,0:T(8,128)(2,1)S(1)}, bf16[512,512]{1,0:T(8,128)(2,1)}, u32[]{:S(2)}) copy-start(bf16[512,512]{1,0:T(8,128)(2,1)} %param.8) | copy-start | bytes 1572868
  4.4 14.7 %all-to-all-start = ((s32[32,1,6]{2,1,0:T(1,128)}), s32[32,1,6]{2,1,0:T(1,128)S(1)}, u32[]{:S(2)}, u32[]{:S(2)}) async-start(s32[32,1,6]{2,1,0:T(1,128)} %copy.58), calls=%async_computation | async-start | bytes 32768 | tf_op jit(solution)/shard_map/all_to_all | solution.py:52
  27.1 83.2 %all-to-all-start.1 = ((bf16[32,6,128,128]{3,2,1,0:T(8,128)(2,1)}), bf16[32,6,128,128]{3,2,1,0:T(8,128)(2,1)}, u32[]{:S(2)}, u32[]{:S(2)}) async-start(bf16[32,6,128,128]{3,2,1,0:T(8,128)(2,1)} %bitcast.100), calls=%async_computation.1 | async-start | bytes 12582912 | tf_op jit(solution)/shard_map/all_to_all | solution.py:60
  317.6 10.4 %slice-start = ((bf16[216,128,128]{2,1,0:T(8,128)(2,1)}), bf16[24,128,128]{2,1,0:T(8,128)(2,1)S(1)}, s32[]{:S(2)}) async-start(bf16[216,128,128]{2,1,0:T(8,128)(2,1)} %convert.10), calls=%async_computation.9 | async-start | bytes 1572864 | tf_op jit(solution)/shard_map/slice | solution.py:87
  317.6 86.9 %all-to-all-start.4 = ((bf16[32,6,128,128]{3,2,1,0:T(8,128)(2,1)}), bf16[32,6,128,128]{3,2,1,0:T(8,128)(2,1)}, u32[]{:S(2)}, u32[]{:S(2)}) async-start(bf16[32,6,128,128]{3,2,1,0:T(8,128)(2,1)} %bitcast.101), calls=%async_computation.4 | async-start | bytes 12582912 | tf_op jit(solution)/shard_map/all_to_all | solution.py:93
  573.6 1.1 copy-start.1
  734.7 5.1 slice-start.1
  734.7 83.0 %all-to-all-start.8 = ((bf16[32,6,128,128]{3,2,1,0:T(8,128)(2,1)}), bf16[32,6,128,128]{3,2,1,0:T(8,128)(2,1)}, u32[]{:S(2)}, u32[]{:S(2)}) async-start(bf16[32,6,128,128]{3,2,1,0:T(8,128)(2,1)} %bitcast.102), calls=%async_computation.8 | async-start | bytes 12582912 | tf_op jit(solution)/shard_map/all_to_all | solution.py:93
